TPU v7x, 512 devices: a whole 4x8x8 slice. The times are simulated.
512 devices in a mesh: req: 32 (over x, y), seq: 16 (over z, core).
Axes of the slice: x: 4, y: 8, z: 8, core: 2. Of those that a mesh axis runs over, the one named last changes fastest.
Arguments:
- q_slots: bfloat16 [65536, 4096], P(('req', 'seq')), parts along dimension 0, may hold values from -240 to 240
- k_cache: bfloat16 [65536, 4096], P(('req', 'seq')), parts along dimension 0, may hold values from -6 to 6
- v_cache: bfloat16 [65536, 4096], P(('req', 'seq')), parts along dimension 0, may hold values from -6 to 6
- tiles: int32 [512, 2], P(('req', 'seq')), parts along dimension 0, may hold values from -1 to 1, as said below
Outputs:
- refreshed: bfloat16 [65536, 4096], P(('req', 'seq')), parts along dimension 0
There are 32 independent parts, one for each index of `req`. A program takes and returns all parts, laid end to end along the dimension named above; each array names one. Nothing has to cross between parts.
Inputs may be any that keep to these rules, and one draw needn't show every extreme that they name: `tiles`: in each row the live entries come first, distinct and ascending, and the rest are -1. Exactly 12 entries of a request are live, and some index of seq has all 2 slots live.
All inputs are finite; a program needn't handle non-finite values.
Results may differ from a plain program's by a relative error of at most 0.02.
The roundings to bfloat16 on the way count: a program that leaves them out, or rounds other values in their place, can miss the bound.
Values may be sent and summed in bfloat16 or wider, within the bound.
A program may use at most 64 MiB of HBM per device.

v0:
```python
import jax
import jax.numpy as jnp
from jax import lax
from jax.sharding import PartitionSpec as P

DH = 128


def rotate(values, position):
    half_dim = DH // 2
    inverse = 10000.0 ** (-jnp.arange(half_dim, dtype=jnp.float32) / half_dim)
    angles = position[..., None, None] * inverse
    cosine = jnp.cos(angles)
    sine = jnp.sin(angles)
    first = values[..., :half_dim]
    second = values[..., half_dim:]
    return jnp.concatenate(
        [first * cosine - second * sine, second * cosine + first * sine], axis=-1
    )


def attend(queries, key_rows, value_rows):
    row_count, local_width = queries.shape
    local_heads = local_width // DH
    key_three = key_rows.reshape(key_rows.shape[0], local_heads, DH)
    value_three = value_rows.reshape(value_rows.shape[0], local_heads, DH)

    def one_block(block_rows):
        scores = jnp.einsum(
            "qhd,khd->hqk", block_rows, key_three, preferred_element_type=jnp.float32
        ) * DH ** (-0.5)
        largest = jnp.max(scores, axis=-1, keepdims=True)
        expsum = jnp.exp(scores - largest)
        probs = (expsum / jnp.sum(expsum, axis=-1, keepdims=True)).astype(jnp.bfloat16)
        output = jnp.einsum("hqk,khd->qhd", probs, value_three, preferred_element_type=jnp.float32)
        return output.astype(jnp.bfloat16).reshape(block_rows.shape[0], local_width)

    query_three = queries.reshape(row_count, local_heads, DH)
    blocked = query_three.reshape(row_count // 512, 512, local_heads, DH)
    return lax.map(one_block, blocked).reshape(row_count, local_width)


def send_home(result):
    return lax.all_to_all(result, "seq", split_axis=0, concat_axis=2, tiled=True)


def on_device(q_slots, k_cache, v_cache, tiles):
    my_index = lax.axis_index("seq")
    per_dev = tiles.shape[1]
    tile_rows = q_slots.shape[0] // per_dev
    width = q_slots.shape[1]
    key_heads, value_heads = (
        lax.all_to_all(k_cache, "seq", split_axis=1, concat_axis=0, tiled=True),
        lax.all_to_all(v_cache, "seq", split_axis=1, concat_axis=0, tiled=True),
    )
    my_list = tiles[0]
    live = my_list >= 0
    global_tile = my_index * per_dev + jnp.maximum(my_list, 0)
    position = (
        global_tile[:, None] * tile_rows + jnp.arange(tile_rows, dtype=jnp.int32)[None, :]
    ).astype(jnp.float32)
    queries = q_slots.astype(jnp.float32).reshape(per_dev, tile_rows, width // DH, DH)
    rotated = rotate(queries, position).astype(jnp.bfloat16).reshape(per_dev, tile_rows, width)
    arrived = lax.all_to_all(rotated, "seq", split_axis=2, concat_axis=0, tiled=True)
    slot_count, item_rows, local_width = arrived.shape
    flat = arrived.reshape(slot_count * item_rows, local_width)
    result = attend(flat, key_heads, value_heads).reshape(slot_count, item_rows, local_width)
    attended = send_home(result)
    masked = jnp.where(live[:, None, None], attended, jnp.zeros((), jnp.bfloat16))
    return masked.reshape(per_dev * tile_rows, width)


def solution(mesh):
    in_specs = (
        P(("req", "seq"), None),
        P(("req", "seq"), None),
        P(("req", "seq"), None),
        P(("req", "seq"), None),
    )
    out_specs = P(("req", "seq"), None)
    return jax.shard_map(
        on_device, mesh=mesh, in_specs=in_specs, out_specs=out_specs, check_vma=False
    )
```

profile of v0, /device:TPU:1, one launch (start us, length us, event | category | flops | bytes accessed | tf_op | source)
XLA Modules:
  0.0 206.6 jit_solution(9679395299821709892)
XLA Ops:
  0.0 1.4 convert_bitcast_fusion
  1.4 0.4 copy.48
  1.8 2.7 %fusion.12 = (f32[2,64,32,64]{3,2,1,0:T(8,128)}, f32[2,64,32,64]{3,2,1,0:T(8,128)}) fusion(f32[2,64,32,128]{3,2,1,0:T(8,128)S(1)} %bitcast.57), kind=kLoop, calls=%fused_computation.26 | loop fusion | bytes 4194304 | tf_op jit(solution)/shard_map/slice | solution.py:16
  4.5 2.9 %copy.46 = f32[2,64,32,64]{1,0,3,2:T(2,128)S(1)} copy(f32[2,64,32,64]{3,2,1,0:T(8,128)} %get-tuple-element.68) | data formatting | bytes 2097152
  7.5 4.1 %copy.47 = f32[2,64,32,64]{1,0,3,2:T(2,128)} copy(f32[2,64,32,64]{3,2,1,0:T(8,128)} %get-tuple-element.67) | data formatting | bytes 2097152
  11.7 1.1 multiply_cosine_fusion
  12.8 3.4 %subtract_convert_fusion = (bf16[2,64,32,64]{1,0,3,2:T(2,128)(2,1)S(1)}, bf16[2,64,32,64]{1,0,3,2:T(2,128)(2,1)S(1)}) fusion(f32[2,64,32,64]{1,0,3,2:T(2,128)} %copy.47, f32[2,64,32,64]{1,0,3,2:T(2,128)S(1)} %copy.46, f32[2,64,64]{1,0,2:T(2,128)S(1)} %get-tuple-element.70, f32[2,64,64]{1,0,2:T(2,128)S(1)} %get-tuple-element.69), kind=kLoop, calls=%fused_computation.17 | loop fusion | flops 2097152 | bytes 3211264 | tf_op jit(solution)/shard_map/convert.1
  16.2 3.2 %pad_maximum_fusion = bf16[2,64,32,128]{1,0,3,2:T(2,128)(2,1)S(1)} fusion(bf16[2,64,32,64]{1,0,3,2:T(2,128)(2,1)S(1)} %get-tuple-element.66, bf16[2,64,32,64]{1,0,3,2:T(2,128)(2,1)S(1)} %get-tuple-element.65), kind=kLoop, calls=%fused_computation.14 | loop fusion | flops 524288 | bytes 2097152 | tf_op jit(solution)/shard_map/concatenate | solution.py:17
  19.5 2.2 %reshape.96 = bf16[16,2,16384]{2,1,0:T(2,128)(2,1)} reshape(bf16[4096,2,64]{2,1,0:T(2,128)(2,1)S(1)} %bitcast.59) | data formatting | bytes 2097152
  21.7 12.0 %all-to-all-start = ((bf16[16,2,16384]{2,1,0:T(2,128)(2,1)}), bf16[16,2,16384]{2,1,0:T(2,128)(2,1)S(1)}, u32[]{:S(2)}, u32[]{:S(2)}) async-start(bf16[16,2,16384]{2,1,0:T(2,128)(2,1)} %reshape.96), calls=%async_computation | async-start | bytes 2097152 | tf_op jit(solution)/shard_map/all_to_all | solution.py:64
  33.7 1.3 copy.33
  35.0 26.6 %all-to-all-done = bf16[16,2,16384]{2,1,0:T(2,128)(2,1)S(1)} async-done(((bf16[16,2,16384]{2,1,0:T(2,128)(2,1)}), bf16[16,2,16384]{2,1,0:T(2,128)(2,1)S(1)}, u32[]{:S(2)}, u32[]{:S(2)}) %all-to-all-start) | async-done | bytes 1048608 | tf_op jit(solution)/shard_map/all_to_all | solution.py:64
  61.6 3.6 %all-to-all-start.1 = ((bf16[128,16,256]{0,2,1:T(8,128)(2,1)}), bf16[128,16,256]{0,2,1:T(8,128)(2,1)S(1)}, u32[]{:S(2)}, u32[]{:S(2)}) async-start(bf16[128,16,256]{0,2,1:T(8,128)(2,1)} %bitcast.9), calls=%async_computation.1 | async-start | bytes 2097152 | tf_op jit(solution)/shard_map/all_to_all | solution.py:53
  65.2 1.3 copy.35
  66.5 26.6 %all-to-all-done.1 = bf16[128,16,256]{0,2,1:T(8,128)(2,1)S(1)} async-done(((bf16[128,16,256]{0,2,1:T(8,128)(2,1)}), bf16[128,16,256]{0,2,1:T(8,128)(2,1)S(1)}, u32[]{:S(2)}, u32[]{:S(2)}) %all-to-all-start.1) | async-done | bytes 1048608 | tf_op jit(solution)/shard_map/all_to_all | solution.py:53
  93.1 4.4 %all-to-all-start.2 = ((bf16[128,16,256]{0,2,1:T(8,128)(2,1)}), bf16[128,16,256]{0,2,1:T(8,128)(2,1)}, u32[]{:S(2)}, u32[]{:S(2)}) async-start(bf16[128,16,256]{0,2,1:T(8,128)(2,1)} %bitcast.11), calls=%async_computation.2 | async-start | bytes 2097152 | tf_op jit(solution)/shard_map/all_to_all | solution.py:54
  97.5 1.3 reshape.97
  98.9 3.4 %copy.42 = bf16[2,64,16,256]{3,1,0,2:T(8,128)(2,1)} copy(bf16[2,64,16,256]{1,0,3,2:T(2,128)(2,1)S(1)} %bitcast.58) | data formatting | bytes 2097152 | tf_op jit(solution)/shard_map/all_to_all | solution.py:64
  102.3 1.4 reshape_reshape_reshape.3
  103.8 0.7 copy.34
  104.5 0.5 reshape.91
  105.0 0.7 copy.38
  105.7 19.0 %all-to-all-done.2 = bf16[128,16,256]{0,2,1:T(8,128)(2,1)} async-done(((bf16[128,16,256]{0,2,1:T(8,128)(2,1)}), bf16[128,16,256]{0,2,1:T(8,128)(2,1)}, u32[]{:S(2)}, u32[]{:S(2)}) %all-to-all-start.2) | async-done | bytes 1048608 | tf_op jit(solution)/shard_map/all_to_all | solution.py:54
  124.6 1.9 copy.36
  126.6 1.3 reshape.92
  127.9 45.1 %while.10 = (s32[]{:T(128)}, bf16[4,512,256]{2,1,0:T(8,128)(2,1)}, bf16[4,512,2,128]{3,2,1,0:T(2,128)(2,1)S(1)}, bf16[2048,2,128]{2,0,1:T(8,128)(2,1)S(1)}, bf16[2048,2,128]{0,2,1:T(8,128)(2,1)}, /*index=5*/s32[]{:T(128)}) while((s32[]{:T(128)}, bf16[4,512,256]{2,1,0:T(8,128)(2,1)}, bf16[4,512,2,128]{3,2,1,0:T(2,128)(2,1)S(1)}, ...), condition=%wide.region_3.4_spmd, body=%wide.region_0.3_spmd.sunk | while | flops 1084360704 | bytes 20980296 | solution.py:40
  127.9 0.2 constant_dynamic-slice_fusion.2
  128.1 5.0 %fusion.22 = (f32[2,512]{1,0:T(2,128)S(1)}, f32[2,512,2048]{2,1,0:T(8,128)}) fusion(bf16[2048,2,128]{2,0,1:T(8,128)(2,1)S(1)} %get-tuple-element.121, bf16[1,512,2,128]{3,2,1,0:T(2,128)(2,1)S(1)} %constant_dynamic-slice_fusion.2), kind=kOutput, calls=%fused_computation.25.clone.1 | convolution fusion | flops 543164416 | bytes 9703424 | tf_op jit(solution)/shard_map/while/body/eval_jaxpr/sub | solution.py:33
  133.1 5.2 %fusion.23 = bf16[2,512,128]{1,2,0:T(8,128)(2,1)S(1)} fusion(bf16[2048,2,128]{0,2,1:T(8,128)(2,1)} %get-tuple-element.122, f32[2,512,2048]{2,1,0:T(8,128)} %get-tuple-element.104, f32[2,512]{1,0:T(2,128)S(1)} %get-tuple-element.105), kind=kOutput, calls=%fused_computation.7.clone.1 | convolution fusion | flops 541196288 | bytes 9703424 | tf_op jit(solution)/shard_map/while/body/eval_jaxpr/hqk,khd->qhd/dot_general | solution.py:35
  138.4 0.7 constant_dynamic-update-slice_fusion.2
  139.2 0.2 constant_dynamic-slice_fusion.2
  139.3 5.0 %fusion.22 = (f32[2,512]{1,0:T(2,128)S(1)}, f32[2,512,2048]{2,1,0:T(8,128)}) fusion(bf16[2048,2,128]{2,0,1:T(8,128)(2,1)S(1)} %get-tuple-element.121, bf16[1,512,2,128]{3,2,1,0:T(2,128)(2,1)S(1)} %constant_dynamic-slice_fusion.2), kind=kOutput, calls=%fused_computation.25.clone.1 | convolution fusion | flops 543164416 | bytes 9703424 | tf_op jit(solution)/shard_map/while/body/eval_jaxpr/sub | solution.py:33
  144.4 5.2 %fusion.23 = bf16[2,512,128]{1,2,0:T(8,128)(2,1)S(1)} fusion(bf16[2048,2,128]{0,2,1:T(8,128)(2,1)} %get-tuple-element.122, f32[2,512,2048]{2,1,0:T(8,128)} %get-tuple-element.104, f32[2,512]{1,0:T(2,128)S(1)} %get-tuple-element.105), kind=kOutput, calls=%fused_computation.7.clone.1 | convolution fusion | flops 541196288 | bytes 9703424 | tf_op jit(solution)/shard_map/while/body/eval_jaxpr/hqk,khd->qhd/dot_general | solution.py:35
  149.6 0.1 copy.64
  149.7 0.7 constant_dynamic-update-slice_fusion.2
  150.4 0.2 constant_dynamic-slice_fusion.2
  150.6 5.0 %fusion.22 = (f32[2,512]{1,0:T(2,128)S(1)}, f32[2,512,2048]{2,1,0:T(8,128)}) fusion(bf16[2048,2,128]{2,0,1:T(8,128)(2,1)S(1)} %get-tuple-element.121, bf16[1,512,2,128]{3,2,1,0:T(2,128)(2,1)S(1)} %constant_dynamic-slice_fusion.2), kind=kOutput, calls=%fused_computation.25.clone.1 | convolution fusion | flops 543164416 | bytes 9703424 | tf_op jit(solution)/shard_map/while/body/eval_jaxpr/sub | solution.py:33
  155.6 5.2 %fusion.23 = bf16[2,512,128]{1,2,0:T(8,128)(2,1)S(1)} fusion(bf16[2048,2,128]{0,2,1:T(8,128)(2,1)} %get-tuple-element.122, f32[2,512,2048]{2,1,0:T(8,128)} %get-tuple-element.104, f32[2,512]{1,0:T(2,128)S(1)} %get-tuple-element.105), kind=kOutput, calls=%fused_computation.7.clone.1 | convolution fusion | flops 541196288 | bytes 9703424 | tf_op jit(solution)/shard_map/while/body/eval_jaxpr/hqk,khd->qhd/dot_general | solution.py:35
  161.0 0.7 constant_dynamic-update-slice_fusion.2
  161.7 0.2 constant_dynamic-slice_fusion.2
  161.9 5.0 %fusion.22 = (f32[2,512]{1,0:T(2,128)S(1)}, f32[2,512,2048]{2,1,0:T(8,128)}) fusion(bf16[2048,2,128]{2,0,1:T(8,128)(2,1)S(1)} %get-tuple-element.121, bf16[1,512,2,128]{3,2,1,0:T(2,128)(2,1)S(1)} %constant_dynamic-slice_fusion.2), kind=kOutput, calls=%fused_computation.25.clone.1 | convolution fusion | flops 543164416 | bytes 9703424 | tf_op jit(solution)/shard_map/while/body/eval_jaxpr/sub | solution.py:33
  166.9 5.2 %fusion.23 = bf16[2,512,128]{1,2,0:T(8,128)(2,1)S(1)} fusion(bf16[2048,2,128]{0,2,1:T(8,128)(2,1)} %get-tuple-element.122, f32[2,512,2048]{2,1,0:T(8,128)} %get-tuple-element.104, f32[2,512]{1,0:T(2,128)S(1)} %get-tuple-element.105), kind=kOutput, calls=%fused_computation.7.clone.1 | convolution fusion | flops 541196288 | bytes 9703424 | tf_op jit(solution)/shard_map/while/body/eval_jaxpr/hqk,khd->qhd/dot_general | solution.py:35
  172.3 0.7 constant_dynamic-update-slice_fusion.2
  173.0 3.6 %all-to-all-start.3 = ((bf16[32,64,256]{2,1,0:T(8,128)(2,1)}), bf16[32,64,256]{2,1,0:T(8,128)(2,1)S(1)}, u32[]{:S(2)}, u32[]{:S(2)}) async-start(bf16[32,64,256]{2,1,0:T(8,128)(2,1)} %bitcast.66), calls=%async_computation.3 | async-start | bytes 2097152 | tf_op jit(solution)/shard_map/all_to_all | solution.py:44
  176.7 27.7 %all-to-all-done.3 = bf16[32,64,256]{2,1,0:T(8,128)(2,1)S(1)} async-done(((bf16[32,64,256]{2,1,0:T(8,128)(2,1)}), bf16[32,64,256]{2,1,0:T(8,128)(2,1)S(1)}, u32[]{:S(2)}, u32[]{:S(2)}) %all-to-all-start.3) | async-done | bytes 1048608 | tf_op jit(solution)/shard_map/all_to_all | solution.py:44
  204.5 0.6 copy.40
  205.1 0.4 copy.49
  205.5 1.1 broadcast_select_fusion
  (20 shorter events, 0.8 us)
Async XLA Ops:
  7.4 4.1 %copy-start.4 = (s32[1,2]{1,0:T(1,128)S(1)}, s32[1,2]{1,0:T(1,128)}, u32[]{:S(2)}) copy-start(s32[1,2]{1,0:T(1,128)} %param.9) | copy-start | bytes 28
  21.7 12.0 %copy-start.2 = (bf16[128,4096]{1,0:T(8,128)(2,1)S(1)}, bf16[128,4096]{1,0:T(8,128)(2,1)}, u32[]{:S(2)}) copy-start(bf16[128,4096]{1,0:T(8,128)(2,1)} %param.7) | copy-start | bytes 3145732
  21.7 39.9 %all-to-all-start = ((bf16[16,2,16384]{2,1,0:T(2,128)(2,1)}), bf16[16,2,16384]{2,1,0:T(2,128)(2,1)S(1)}, u32[]{:S(2)}, u32[]{:S(2)}) async-start(bf16[16,2,16384]{2,1,0:T(2,128)(2,1)} %reshape.96), calls=%async_computation | async-start | bytes 2097152 | tf_op jit(solution)/shard_map/all_to_all | solution.py:64
  33.7 31.5 %copy-start.3 = (bf16[128,4096]{1,0:T(8,128)(2,1)S(1)}, bf16[128,4096]{1,0:T(8,128)(2,1)}, u32[]{:S(2)}) copy-start(bf16[128,4096]{1,0:T(8,128)(2,1)} %param.8) | copy-start | bytes 3145732
  61.6 31.5 %all-to-all-start.1 = ((bf16[128,16,256]{0,2,1:T(8,128)(2,1)}), bf16[128,16,256]{0,2,1:T(8,128)(2,1)S(1)}, u32[]{:S(2)}, u32[]{:S(2)}) async-start(bf16[128,16,256]{0,2,1:T(8,128)(2,1)} %bitcast.9), calls=%async_computation.1 | async-start | bytes 2097152 | tf_op jit(solution)/shard_map/all_to_all | solution.py:53
  93.1 4.4 %copy-start = (bf16[128,16,256]{0,2,1:T(8,128)(2,1)}, bf16[128,16,256]{0,2,1:T(8,128)(2,1)S(1)}, u32[]{:S(2)}) copy-start(bf16[128,16,256]{0,2,1:T(8,128)(2,1)S(1)} %all-to-all-done.1) | copy-start | bytes 3145732
  93.1 31.6 %all-to-all-start.2 = ((bf16[128,16,256]{0,2,1:T(8,128)(2,1)}), bf16[128,16,256]{0,2,1:T(8,128)(2,1)}, u32[]{:S(2)}, u32[]{:S(2)}) async-start(bf16[128,16,256]{0,2,1:T(8,128)(2,1)} %bitcast.11), calls=%async_computation.2 | async-start | bytes 2097152 | tf_op jit(solution)/shard_map/all_to_all | solution.py:54
  102.3 1.5 copy-start.1
  173.0 31.5 %all-to-all-start.3 = ((bf16[32,64,256]{2,1,0:T(8,128)(2,1)}), bf16[32,64,256]{2,1,0:T(8,128)(2,1)S(1)}, u32[]{:S(2)}, u32[]{:S(2)}) async-start(bf16[32,64,256]{2,1,0:T(8,128)(2,1)} %bitcast.66), calls=%async_computation.3 | async-start | bytes 2097152 | tf_op jit(solution)/shard_map/all_to_all | solution.py:44
where the time goes:
time: 207 us
  waiting for transfers between devices  99.9 us (48%)
  matrix products  40.9 us (20%)
  local copies, waits for them, and re-layouts  31.7 us (15%)
  starting transfers between devices  23.5 us (11%)
  other arithmetic  10.4 us (5%)
    all_to_all x1, waiting for transfers between devices, send_home(): lax.all_to_all(result, 'seq', split_axis=0, concat_axis=2, tiled=True)  27.7 us
    all_to_all x1, waiting for transfers between devices, on_device(): lax.all_to_all(rotated, 'seq', split_axis=2, concat_axis=0, tiled=True)  26.6 us
    all_to_all x1, waiting for transfers between devices, on_device(): lax.all_to_all(k_cache, 'seq', split_axis=1, concat_axis=0, tiled=True)  26.6 us
    dot_general x4, matrix products, one_block(): jnp.einsum('hqk,khd->qhd', probs, value_three, preferred_element_type=jnp...  20.8 us
    sub x4, matrix products, one_block(): expsum = jnp.exp(scores - largest)  20.1 us
    all_to_all x1, waiting for transfers between devices, on_device(): lax.all_to_all(v_cache, 'seq', split_axis=1, concat_axis=0, tiled=True)  19 us
    unnamed x18, local copies, waits for them, and re-layouts  14.2 us
    all_to_all x1, starting transfers between devices, on_device(): lax.all_to_all(rotated, 'seq', split_axis=2, concat_axis=0, tiled=True)  12 us
  transfers between devices with their start and end apart: 4, of which 4 were waited for; matrix products, arithmetic and copies ran while one was open for 5% of the time, Pallas kernels for 0%

commit v1 on v0

v1 whole, which is shorter than its diff:
```python
import functools
import math

import jax
import jax.numpy as jnp
import numpy as np
from jax import lax
from jax.experimental import pallas as pl
from jax.experimental.pallas import tpu as pltpu
from jax.sharding import PartitionSpec as P

MESH = pl.DeviceIdType.MESH
DH = 128


def kernel(n, tiles_ref, inv_ref, q_ref, k_ref, v_ref, o_ref,
           q_in, q_rot, q_all, k_all, v_all, probs, norm, o_send,
           local_sem, k_send, k_recv, v_send, v_recv, q_send, q_recv, o_ssem, o_rsem):
    me = lax.axis_index("seq")
    rows, width = q_in.shape
    local = width // n
    heads = local // DH
    tile_rows = rows // 2
    keys = n * rows

    def cols(index):
        return pl.ds(pl.multiple_of(index * local, local), local)

    def span(index):
        return pl.ds(pl.multiple_of(index * rows, rows), rows)

    def peer(offset):
        return lax.rem(me + offset, n)

    barrier = pltpu.get_barrier_semaphore()
    for offset in range(1, n):
        pl.semaphore_signal(barrier, inc=1, device_id={"seq": peer(offset)}, device_id_type=MESH)
    load_q = pltpu.make_async_copy(q_ref, q_in, local_sem.at[0])
    load_q.start()
    own_k = pltpu.make_async_copy(k_ref.at[:, cols(me)], k_all.at[span(me), :], local_sem.at[1])
    own_k.start()
    own_v = pltpu.make_async_copy(v_ref.at[:, cols(me)], v_all.at[span(me), :], local_sem.at[2])
    own_v.start()
    pl.semaphore_wait(barrier, n - 1)

    def send(source, target, send_sem, recv_sem, offset):
        to = peer(offset)
        return pltpu.make_async_remote_copy(
            src_ref=source.at[:, cols(to)],
            dst_ref=target.at[span(me), :],
            send_sem=send_sem.at[offset],
            recv_sem=recv_sem.at[offset],
            device_id={"seq": to},
            device_id_type=MESH,
        )

    send_k = functools.partial(send, k_ref, k_all, k_send, k_recv)
    send_v = functools.partial(send, v_ref, v_all, v_send, v_recv)
    send_q = functools.partial(send, q_rot, q_all, q_send, q_recv)

    def send_o(offset):
        to = peer(offset)
        return pltpu.make_async_remote_copy(
            src_ref=o_send.at[span(to), :],
            dst_ref=o_ref.at[:, cols(me)],
            send_sem=o_ssem.at[offset],
            recv_sem=o_rsem.at[offset],
            device_id={"seq": to},
            device_id_type=MESH,
        )

    order = []
    for step in range(1, n // 2 + 1):
        order += [step] if step == n // 2 else [step, n - step]

    for offset in order:
        send_k(offset).start()

    row = lax.broadcasted_iota(jnp.int32, (rows, DH), 0)
    lane = lax.broadcasted_iota(jnp.int32, (rows, DH), 1)
    first = jnp.maximum(tiles_ref[0, 0], 0) * tile_rows
    second = (jnp.maximum(tiles_ref[0, 1], 0) - 1) * tile_rows
    position = (me * rows + row + jnp.where(row < tile_rows, first, second)).astype(jnp.float32)
    angles = position * inv_ref[0:1, :]
    cosine = jnp.cos(angles)
    sine = jnp.where(lane < DH // 2, -jnp.sin(angles), jnp.sin(angles))
    load_q.wait()

    def rotate(head, carry):
        at = pl.ds(pl.multiple_of(head * DH, DH), DH)
        value = q_in[:, at].astype(jnp.float32)
        swapped = pltpu.roll(value, DH // 2, axis=1)
        q_rot[:, at] = (value * cosine + swapped * sine).astype(jnp.bfloat16)
        return carry

    lax.fori_loop(0, width // DH, rotate, 0)
    for offset in order:
        send_q(offset).start()
    for offset in order:
        send_v(offset).start()
    q_all[span(me), :] = q_rot[:, cols(me)]

    own_k.wait()
    for offset in order:
        send_k(offset).wait_recv()

    factor = math.log2(math.e) / math.sqrt(DH)

    def score(offset, carry):
        source = peer(n - offset)

        @pl.when(offset > 0)
        def _():
            send_q(offset).wait_recv()

        for head in range(heads):
            at = pl.ds(head * DH, DH)
            logits = lax.dot_general(
                q_all[span(source), at], k_all[:, at],
                (((1,), (1,)), ((), ())), preferred_element_type=jnp.float32,
            )
            largest = jnp.max(logits, axis=1, keepdims=True)
            weight = jnp.exp2((logits - largest) * factor)
            norm[span(source), at] = jnp.broadcast_to(
                1.0 / jnp.sum(weight, axis=1, keepdims=True), (rows, DH)
            )
            probs[head, span(source), :] = weight.astype(jnp.bfloat16)
        return carry

    lax.fori_loop(0, n, score, 0)

    own_v.wait()
    for offset in order:
        send_v(offset).wait_recv()

    def combine(step, carry):
        offset = lax.rem(step + 1, n)
        source = peer(offset)
        for head in range(heads):
            at = pl.ds(head * DH, DH)
            total = jnp.dot(
                probs[head, span(source), :], v_all[:, at], preferred_element_type=jnp.float32
            )
            o_send[span(source), at] = (total * norm[span(source), at]).astype(jnp.bfloat16)

        @pl.when(offset > 0)
        def _():
            send_o(offset).start()

        return carry

    lax.fori_loop(0, n, combine, 0)
    o_ref[:, cols(me)] = o_send[span(me), :]
    for offset in order:
        send_k(offset).wait_send()
        send_q(offset).wait_send()
        send_v(offset).wait_send()
    for offset in order:
        send_o(offset).wait()


def on_device(n, q_slots, k_cache, v_cache, tiles):
    rows, width = q_slots.shape
    local = width // n
    half = DH // 2
    inverse = 10000.0 ** (-np.arange(half) / half)
    inverse = jnp.asarray(np.broadcast_to(np.tile(inverse, 2)[None, :], (8, DH)), jnp.float32)
    dma = pltpu.SemaphoreType.DMA
    attended = pl.pallas_call(
        functools.partial(kernel, n),
        out_shape=jax.ShapeDtypeStruct((rows, width), jnp.bfloat16),
        in_specs=[
            pl.BlockSpec(memory_space=pltpu.SMEM),
            pl.BlockSpec(memory_space=pltpu.VMEM),
            pl.BlockSpec(memory_space=pl.ANY),
            pl.BlockSpec(memory_space=pl.ANY),
            pl.BlockSpec(memory_space=pl.ANY),
        ],
        out_specs=pl.BlockSpec(memory_space=pltpu.VMEM),
        scratch_shapes=[
            pltpu.VMEM((rows, width), jnp.bfloat16),
            pltpu.VMEM((rows, width), jnp.bfloat16),
            pltpu.VMEM((n * rows, local), jnp.bfloat16),
            pltpu.VMEM((n * rows, local), jnp.bfloat16),
            pltpu.VMEM((n * rows, local), jnp.bfloat16),
            pltpu.VMEM((local // DH, n * rows, n * rows), jnp.bfloat16),
            pltpu.VMEM((n * rows, local), jnp.float32),
            pltpu.VMEM((n * rows, local), jnp.bfloat16),
            dma((3,)),
        ] + [dma((n,))] * 8,
        name="refresh_attention",
        compiler_params=pltpu.CompilerParams(
            collective_id=0, has_side_effects=True, vmem_limit_bytes=56 * 2**20
        ),
    )(tiles, inverse, q_slots, k_cache, v_cache)
    live = jnp.repeat(tiles[0] >= 0, rows // tiles.shape[1])
    return jnp.where(live[:, None], attended, jnp.zeros((), jnp.bfloat16))


def solution(mesh):
    spec = P(("req", "seq"), None)
    return jax.shard_map(
        functools.partial(on_device, mesh.shape["seq"]),
        mesh=mesh, in_specs=(spec,) * 4, out_specs=spec, check_vma=False,
    )
```

time: 207 us -> 113 us (0.55)
  Pallas kernels: 0 us -> 110 us
  waiting for transfers between devices: 99.9 us -> 0 us
  matrix products: 40.9 us -> 0 us
  local copies, waits for them, and re-layouts: 31.7 us -> 0.16 us
  starting transfers between devices: 23.5 us -> 0 us
  other arithmetic: 10.4 us -> 2.99 us
    pallas_call x0 -> x1, Pallas kernels: none -> 110 us  [on_device(): pl.pallas_call(functools.partial(kernel, n), out_shape=jax.ShapeDtypeStru...]
    all_to_all x4 -> x0, waiting for transfers between devices: 99.9 us -> none  [the longest x1 27.7 us: send_home(): lax.all_to_all(result, 'seq', split_axis=0, concat_axis=2, tiled=True)]
    all_to_all x4 -> x0, starting transfers between devices: 23.5 us -> none  [the longest x1 12 us: on_device(): lax.all_to_all(rotated, 'seq', split_axis=2, concat_axis=0, tiled=True)]
    dot_general x4 -> x0, matrix products: 20.8 us -> none  [one_block(): jnp.einsum('hqk,khd->qhd', probs, value_three, preferred_element_type=jnp...]
    sub x4 -> x0, matrix products: 20.1 us -> none  [one_block(): expsum = jnp.exp(scores - largest)]
    unnamed x18 -> x0, local copies, waits for them, and re-layouts: 14.2 us -> none
    all_to_all x4 -> x0, local copies, waits for them, and re-layouts: 6.55 us -> none  [the longest x1 3.38 us: on_device(): lax.all_to_all(rotated, 'seq', split_axis=2, concat_axis=0, tiled=True)]
    another operation x1 -> x0, other arithmetic: 3.45 us -> none
  transfers between devices with their start and end apart: 4 -> 0, of which waited for: 4 -> 0; matrix products, arithmetic and copies ran while one was open for 5% -> 0% of each run, Pallas kernels for 0% -> 0%
where the time goes in v1:
time: 113 us
  Pallas kernels  110 us (97%)
  other arithmetic  2.99 us (3%)
    pallas_call x1, Pallas kernels, on_device(): pl.pallas_call(functools.partial(kernel, n), out_shape=jax.ShapeDtypeStru...  110 us
    select_n x1, other arithmetic, on_device(): return jnp.where(live[:, None], attended, jnp.zeros((), jnp.bfloat16))  2.34 us

profile of v1, /device:TPU:1, one launch (start us, length us, event | category | flops | bytes accessed | tf_op | source)
XLA Modules:
  0.0 113.2 jit_solution(17718979799344064443)
XLA Ops:
  0.0 0.7 compare_bitcast_fusion
  0.7 0.1 broadcast_in_dim.17
  0.7 0.1 broadcast_in_dim.18
  0.8 110.1 %refresh_attention.1 = bf16[128,4096]{1,0:T(8,128)(2,1)} custom-call(s32[1,2]{1,0:T(1,128)} %tiles_ref.1, f32[8,128]{1,0:T(8,128)} %constant.6.clone.inv_ref, bf16[128,4096]{1,0:T(8,128)(2,1)} %q_ref.1, bf16[128,4096]{1,0:T(8,128)(2,1)} %k_ref.1, bf16[128,4096]{1,0:T(8,128)(2,1)} %v_ref.1), custom_call_target="tpu_custom_call" | custom-call | tf_op jit(solution)/shard_map/refresh_attention/pallas_call | solution.py:169
  110.9 2.3 %broadcast_select_fusion = bf16[128,4096]{1,0:T(8,128)(2,1)} fusion(bf16[128,4096]{1,0:T(8,128)(2,1)} %refresh_attention.1, pred[128]{0:T(512)(128)(4,1)S(1)} %broadcast_in_dim.18), kind=kLoop, calls=%fused_computation | loop fusion | flops 524288 | bytes 2097280 | tf_op jit(solution)/shard_map/jit(_where)/select_n | solution.py:197

commit v2 on v0

v2 whole, which is shorter than its diff:
```python
import functools
import math

import jax
import jax.numpy as jnp
import numpy as np
from jax import lax
from jax.experimental import pallas as pl
from jax.experimental.layout import Layout, with_layout_constraint
from jax.experimental.pallas import tpu as pltpu
from jax.sharding import PartitionSpec as P

MESH = pl.DeviceIdType.MESH
DH = 128
HALF = DH // 2
TILE = 64
SLOTS = 2
LIVE = 12
HEADS = 2
LOCAL = HEADS * DH
N = 16
CHIPS = N // 2
ROWS = SLOTS * TILE
ROOM = {1: 8, 2: 6, 3: 5, 4: 3, 5: 1, 6: 0, 7: 0}
HOPS = 5
PACE = (12, 4, 4, 4, 4, 4)


def kernel(tiles_ref, inv_ref, q_ref, k_ref, v_ref, o_ref, flag_ref,
           q_in, q_out, q_chip, q_live, k_all, v_all, probs, norm, o_live, o_send,
           count_out, count_all, counts,
           pack_a, pack_b, land_a, land_b,
           local_sem, count_ssem, count_rsem, twin_ssem, twin_rsem,
           hop_ssem, hop_rsem, k_ssem, k_rsem, v_ssem, v_rsem, o_ssem, o_rsem):
    me = lax.axis_index("seq")
    chip = me // 2
    core = lax.rem(me, 2)

    def at(index, size):
        return pl.ds(pl.multiple_of(index * size, size), size)

    def peer(offset):
        return lax.rem(me + offset, N)

    def remote(source, target, ssem, rsem, **where):
        return pltpu.make_async_remote_copy(
            src_ref=source, dst_ref=target, send_sem=ssem, recv_sem=rsem,
            device_id=where, device_id_type=MESH,
        )

    barrier = pltpu.get_barrier_semaphore()
    for offset in range(1, N):
        pl.semaphore_signal(barrier, inc=1, device_id={"seq": peer(offset)}, device_id_type=MESH)
    load_q = pltpu.make_async_copy(q_ref, q_in, local_sem.at[0])
    load_q.start()
    own_k = pltpu.make_async_copy(k_ref.at[:, at(me, LOCAL)], k_all.at[at(me, ROWS), :], local_sem.at[1])
    own_k.start()
    own_v = pltpu.make_async_copy(v_ref.at[:, at(me, LOCAL)], v_all.at[at(me, ROWS), :], local_sem.at[2])
    own_v.start()

    first_live = (tiles_ref[0, 0] >= 0).astype(jnp.int32)
    second_live = (tiles_ref[0, 1] >= 0).astype(jnp.int32)
    count = jnp.full((8, DH), first_live + second_live, jnp.int32)
    count_out[...] = count
    count_all[me] = count
    pl.semaphore_wait(barrier, N - 1)

    def send_count(offset):
        return remote(count_out, count_all.at[me], count_ssem.at[offset], count_rsem.at[offset], seq=peer(offset))

    def send_k(offset):
        to = peer(offset)
        return remote(k_ref.at[:, at(to, LOCAL)], k_all.at[at(me, ROWS), :],
                      k_ssem.at[offset], k_rsem.at[offset], seq=to)

    def send_v(head, offset):
        to = peer(offset)
        return remote(v_ref.at[:, at(to * HEADS + head, DH)], v_all.at[at(me, ROWS), pl.ds(head * DH, DH)],
                      v_ssem.at[head, offset], v_rsem.at[head, offset], seq=to)

    def send_o(head, offset):
        to = peer(offset)
        return remote(o_send.at[offset, :, pl.ds(head * DH, DH)], o_ref.at[:, at(me * HEADS + head, DH)],
                      o_ssem.at[head, offset], o_rsem.at[head, offset], seq=to)

    order = []
    for step in range(1, N // 2 + 1):
        order += [step] if step == N // 2 else [step, N - step]
    bulk = [send_k(offset) for offset in order]
    bulk += [send_v(head, offset) for head in range(HEADS) for offset in order]
    started = 0

    def start_bulk(amount):
        nonlocal started
        for copy in bulk[started:started + amount]:
            copy.start()
        started += amount

    for offset in order:
        send_count(offset).start()
    start_bulk(PACE[0])

    row = lax.broadcasted_iota(jnp.int32, (ROWS, DH), 0)
    lane = lax.broadcasted_iota(jnp.int32, (ROWS, DH), 1)
    first = jnp.maximum(tiles_ref[0, 0], 0) * TILE
    second = (jnp.maximum(tiles_ref[0, 1], 0) - 1) * TILE
    position = (me * ROWS + row + jnp.where(row < TILE, first, second)).astype(jnp.float32)
    angles = position * inv_ref[0:1, :]
    cosine = jnp.cos(angles)
    sine = jnp.sin(angles)
    sine = jnp.where(lane < HALF, -sine, sine)
    load_q.wait()

    def rotate(plane, target, index, carry):
        head = (index // HEADS * 2 + plane) * HEADS + lax.rem(index, HEADS)
        value = q_in[:, at(head, DH)].astype(jnp.float32)
        swapped = pltpu.roll(value, HALF, axis=1)
        turned = (value * cosine + swapped * sine).astype(jnp.bfloat16)
        for slot in range(SLOTS):
            target[slot, :, at(index, DH)] = turned[slot * TILE:(slot + 1) * TILE, :]
        return carry

    mine = q_chip.at[pl.ds(core * SLOTS, SLOTS)]
    lax.fori_loop(0, CHIPS * HEADS, functools.partial(rotate, 1 - core, q_out), 0)
    twin = remote(q_out, mine, twin_ssem.at[0], twin_rsem.at[0], seq=chip * 2 + 1 - core)
    twin.start()
    lax.fori_loop(0, CHIPS * HEADS, functools.partial(rotate, core, mine), 0)

    for offset in order:
        send_count(offset).wait_recv()
    to_scalar = pltpu.make_async_copy(count_all, counts, local_sem.at[3])
    to_scalar.start()
    to_scalar.wait()

    def count_of(offset, which):
        return counts[lax.rem(chip + offset, CHIPS) * 2 + which, 0, 0]

    first_core = [count_of(offset, 0) for offset in range(CHIPS)]
    there = [first_core[offset] + count_of(offset, 1) for offset in range(CHIPS)]
    below, above, by_a, by_b, total = [], [], [], [], []
    misfit = jnp.int32(0)
    for to in range(CHIPS):
        near_a, near_b = [jnp.int32(0)], [jnp.int32(0)]
        for away in range(1, CHIPS):
            near_a.append(near_a[-1] + there[(to - away) % CHIPS])
            near_b.append(near_b[-1] + there[(to + away) % CHIPS])
        whole = near_a[-1]
        fit_a = fit_b = whole
        for away in range(1, CHIPS):
            fit_a = jnp.minimum(fit_a, near_a[away - 1] + ROOM[away])
            fit_b = jnp.minimum(fit_b, near_b[away - 1] + ROOM[away])
        misfit = jnp.maximum(misfit, whole - fit_a - fit_b)
        below.append(near_a)
        above.append(near_b)
        by_a.append(fit_a)
        by_b.append(whole - fit_a)
        total.append(whole)

    flag_ref[0] = misfit

    def tile_at(rank):
        index = jnp.where(rank < first_core[0], rank, rank + SLOTS - first_core[0])
        return jnp.clip(index, 0, 2 * SLOTS - 1)

    def hop_a(hops):
        return remote(pack_a.at[pl.ds(hops * 8, ROOM[hops])], land_a.at[pl.ds(hops * 8, ROOM[hops])],
                      hop_ssem.at[0, hops], hop_rsem.at[0, hops], seq=peer(2))

    def hop_b(hops):
        return remote(pack_b.at[pl.ds(hops * 8, ROOM[hops])], land_b.at[pl.ds(hops * 8, ROOM[hops])],
                      hop_ssem.at[1, hops], hop_rsem.at[1, hops], seq=peer(N - 2))

    twin.wait_recv()
    for hops in range(HOPS, 0, -1):
        if hops < HOPS:
            hop_a(hops + 1).wait_recv()
            hop_b(hops + 1).wait_recv()
        to_a, to_b = hops, CHIPS - hops
        column_a = at(lax.rem(chip + to_a, CHIPS), LOCAL)
        column_b = at(lax.rem(chip + to_b, CHIPS), LOCAL)
        for slot in range(ROOM[hops]):
            rank = by_a[to_a] - 1 - slot - below[to_a][hops - 1]
            value = q_chip[tile_at(rank), :, column_a]
            if slot < ROOM[hops + 1]:
                is_mine = jnp.logical_and(rank >= 0, rank < there[0])
                value = jnp.where(is_mine, value, land_a[(hops + 1) * 8 + slot])
            pack_a[hops * 8 + slot] = value
            rank = by_b[to_b] - 1 - slot - above[to_b][hops - 1]
            value = q_chip[tile_at(there[0] - 1 - rank), :, column_b]
            if slot < ROOM[hops + 1]:
                is_mine = jnp.logical_and(rank >= 0, rank < there[0])
                value = jnp.where(is_mine, value, land_b[(hops + 1) * 8 + slot])
            pack_b[hops * 8 + slot] = value
        hop_a(hops).start()
        hop_b(hops).start()
        start_bulk(PACE[HOPS + 1 - hops])
    start_bulk(len(bulk) - started)

    hop_a(1).wait_recv()
    hop_b(1).wait_recv()
    column = at(chip, LOCAL)
    for slot in range(LIVE):
        value = q_chip[tile_at(slot - total[0]), :, column]
        other = land_b[8 + jnp.clip(slot - by_a[0], 0, 7)]
        value = jnp.where(slot < total[0], other, value)
        if slot < ROOM[1]:
            value = jnp.where(slot < by_a[0], land_a[8 + slot], value)
        q_live[slot * TILE:(slot + 1) * TILE, :] = value

    own_k.wait()
    for offset in order:
        send_k(offset).wait_recv()

    factor = math.log2(math.e) / math.sqrt(DH)
    block = 2 * TILE

    def score(index, carry):
        for head in range(HEADS):
            columns = pl.ds(head * DH, DH)
            logits = lax.dot_general(
                q_live[at(index, block), columns], k_all[:, columns],
                (((1,), (1,)), ((), ())), preferred_element_type=jnp.float32,
            )
            largest = jnp.max(logits, axis=1, keepdims=True)
            weight = jnp.exp2((logits - largest) * factor)
            norm[at(index, block), columns] = jnp.broadcast_to(
                1.0 / jnp.sum(weight, axis=1, keepdims=True), (block, DH)
            )
            probs[head, at(index, block), :] = weight.astype(jnp.bfloat16)
        return carry

    lax.fori_loop(0, LIVE * TILE // block, score, 0)

    own_v.wait()
    for head in range(HEADS):
        columns = pl.ds(head * DH, DH)
        for offset in order:
            send_v(head, offset).wait_recv()

        def combine(index, carry):
            product = jnp.dot(
                probs[head, at(index, block), :], v_all[:, columns], preferred_element_type=jnp.float32
            )
            product = (product * norm[at(index, block), columns]).astype(jnp.bfloat16)
            for part in range(2):
                o_live[head, index * 2 + part] = product[part * TILE:(part + 1) * TILE, :]
            return carry

        lax.fori_loop(0, LIVE * TILE // block, combine, 0)
        for offset in order + [0]:
            home = peer(offset)
            away = lax.rem(home // 2 - chip + CHIPS, CHIPS)
            which = lax.rem(home, 2)
            back = (CHIPS - away)
            before = jnp.int32(0)
            for step in range(1, CHIPS):
                before = jnp.where(back == step, below[0][step - 1], before)
            rank = jnp.where(which == 0, 0, counts[home // 2 * 2, 0, 0])
            for slot in range(SLOTS):
                index = before + rank + slot
                index = jnp.where(index < by_a[0], by_a[0] - 1 - index, index)
                index = jnp.where(back == CHIPS, total[0] + rank + slot, index)
                o_send[offset, slot * TILE:(slot + 1) * TILE, columns] = o_live[head, jnp.clip(index, 0, LIVE - 1)]
            if offset > 0:
                send_o(head, offset).start()
    o_ref[:, at(me, LOCAL)] = o_send[0]

    for offset in order:
        send_count(offset).wait_send()
    twin.wait_send()
    for hops in range(1, HOPS + 1):
        hop_a(hops).wait_send()
        hop_b(hops).wait_send()
    for copy in bulk:
        copy.wait_send()
    for head in range(HEADS):
        for offset in order:
            send_o(head, offset).wait()
    for slot in range(SLOTS):
        rows = pl.ds(slot * TILE, TILE)
        o_ref[rows, :] = jnp.where(tiles_ref[0, slot] >= 0, o_ref[rows, :], jnp.zeros((), jnp.bfloat16))


def refresh(q_slots, k_cache, v_cache, tiles):
    width = q_slots.shape[1]
    inverse = 10000.0 ** (-np.arange(HALF) / HALF)
    inverse = jnp.asarray(np.broadcast_to(np.tile(inverse, 2)[None, :], (8, DH)), jnp.float32)
    dma = pltpu.SemaphoreType.DMA
    bf16, i32 = jnp.bfloat16, jnp.int32
    unit = (TILE, LOCAL)
    return pl.pallas_call(
        kernel,
        out_shape=(
            jax.ShapeDtypeStruct((ROWS, width), bf16),
            jax.ShapeDtypeStruct((1,), i32),
        ),
        in_specs=[
            pl.BlockSpec(memory_space=pltpu.SMEM),
            pl.BlockSpec(memory_space=pltpu.VMEM),
            pl.BlockSpec(memory_space=pl.ANY),
            pl.BlockSpec(memory_space=pl.ANY),
            pl.BlockSpec(memory_space=pl.ANY),
        ],
        out_specs=(pl.BlockSpec(memory_space=pltpu.VMEM), pl.BlockSpec(memory_space=pltpu.SMEM)),
        scratch_shapes=[
            pltpu.VMEM((ROWS, width), bf16),
            pltpu.VMEM((SLOTS, TILE, width // 2), bf16),
            pltpu.VMEM((2 * SLOTS, TILE, width // 2), bf16),
            pltpu.VMEM((LIVE * TILE, LOCAL), bf16),
            pltpu.VMEM((N * ROWS, LOCAL), bf16),
            pltpu.VMEM((N * ROWS, LOCAL), bf16),
            pltpu.VMEM((HEADS, LIVE * TILE, N * ROWS), bf16),
            pltpu.VMEM((LIVE * TILE, LOCAL), jnp.float32),
            pltpu.VMEM((HEADS, LIVE, TILE, DH), bf16),
            pltpu.VMEM((N, ROWS, LOCAL), bf16),
            pltpu.VMEM((8, DH), i32),
            pltpu.VMEM((N, 8, DH), i32),
            pltpu.SMEM((N, 8, DH), i32),
            pltpu.VMEM(((HOPS + 1) * 8,) + unit, bf16),
            pltpu.VMEM(((HOPS + 1) * 8,) + unit, bf16),
            pltpu.VMEM(((HOPS + 1) * 8,) + unit, bf16),
            pltpu.VMEM(((HOPS + 1) * 8,) + unit, bf16),
            dma((4,)),
            dma((N,)), dma((N,)),
            dma((1,)), dma((1,)),
            dma((2, HOPS + 1)), dma((2, HOPS + 1)),
            dma((N,)), dma((N,)),
            dma((HEADS, N)), dma((HEADS, N)),
            dma((HEADS, N)), dma((HEADS, N)),
        ],
        name="refresh_attention",
        compiler_params=pltpu.CompilerParams(
            collective_id=0, has_side_effects=True, vmem_limit_bytes=56 * 2**20
        ),
    )(tiles, inverse, q_slots, k_cache, v_cache)


def keep_live(attended, tiles):
    row = lax.broadcasted_iota(jnp.int32, attended.shape, 0)
    tile = jnp.where(row < TILE, tiles[0, 0], tiles[0, 1])
    return jnp.where(tile >= 0, attended, jnp.zeros((), attended.dtype))


def every_slot(q_slots, k_cache, v_cache, tiles):
    width = q_slots.shape[1]
    exchange = functools.partial(lax.all_to_all, axis_name="seq", tiled=True)
    keys = exchange(k_cache, split_axis=1, concat_axis=0)
    values = exchange(v_cache, split_axis=1, concat_axis=0)
    tile = lax.axis_index("seq") * SLOTS + jnp.maximum(tiles[0], 0)
    position = (tile[:, None] * TILE + jnp.arange(TILE, dtype=jnp.int32)).reshape(ROWS, 1, 1).astype(jnp.float32)
    angles = position * 10000.0 ** (-jnp.arange(HALF, dtype=jnp.float32) / HALF)
    cosine, sine = jnp.cos(angles), jnp.sin(angles)
    queries = q_slots.astype(jnp.float32).reshape(ROWS, width // DH, DH)
    a, b = queries[..., :HALF], queries[..., HALF:]
    rotated = jnp.concatenate([a * cosine - b * sine, b * cosine + a * sine], axis=-1)
    rotated = rotated.astype(jnp.bfloat16).reshape(ROWS, width)
    rotated = exchange(rotated, split_axis=1, concat_axis=0)

    def one(index):
        head = lax.rem(index, HEADS)
        rows = lax.dynamic_slice(rotated, (index // HEADS * 512, head * DH), (512, DH))
        head_keys = lax.dynamic_slice_in_dim(keys, head * DH, DH, 1)
        head_values = lax.dynamic_slice_in_dim(values, head * DH, DH, 1)
        logits = jnp.dot(rows, head_keys.T, preferred_element_type=jnp.float32) * DH**-0.5
        weight = jnp.exp(logits - jnp.max(logits, axis=-1, keepdims=True))
        weight = (weight / jnp.sum(weight, axis=-1, keepdims=True)).astype(jnp.bfloat16)
        return jnp.dot(weight, head_values, preferred_element_type=jnp.float32).astype(jnp.bfloat16)

    result = lax.map(one, jnp.arange(N * ROWS // 512 * HEADS))
    result = result.reshape(N * ROWS // 512, HEADS, 512, DH).swapaxes(1, 2).reshape(N * ROWS, LOCAL)
    return keep_live(exchange(result, split_axis=0, concat_axis=1), tiles)


def on_device(q_slots, k_cache, v_cache, tiles):
    attended, misfit = refresh(q_slots, k_cache, v_cache, tiles)
    def other_way(carry):
        rowwise = Layout(major_to_minor=(0, 1))
        _, *given = lax.optimization_barrier((carry[0], q_slots, k_cache, v_cache, tiles))
        given = [with_layout_constraint(array, rowwise) for array in given]
        return jnp.int32(0), with_layout_constraint(every_slot(*given), rowwise)

    return lax.while_loop(lambda carry: carry[0] > 0, other_way, (misfit[0], attended))[1]


def solution(mesh):
    spec = P(("req", "seq"), None)
    return jax.shard_map(
        on_device, mesh=mesh, in_specs=(spec,) * 4, out_specs=spec, check_vma=False
    )
```

time: 207 us -> 299 us (1.44)
  the two profiles are of different devices: /device:TPU:1 before, /device:TPU:45 now
where the time goes in v2:
time: 299 us; the launch traced here: 298 us
  waiting for transfers between devices  108 us (36%)
  Pallas kernels  104 us (35%)
  loops' own time  22.9 us (8%)
  matrix products  19.7 us (7%)
  local copies, waits for them, and re-layouts  16 us (5%)
  starting transfers between devices  15.3 us (5%)
  other arithmetic  12.8 us (4%)
    pallas_call x1, Pallas kernels, refresh(): pl.pallas_call(kernel, out_shape=(jax.ShapeDtypeStruct((ROWS, width), bf1...  104 us
    all_to_all x1, waiting for transfers between devices, every_slot(): keys = exchange(k_cache, split_axis=1, concat_axis=0)  27.9 us
    all_to_all x1, waiting for transfers between devices, every_slot(): rotated = exchange(rotated, split_axis=1, concat_axis=0)  26.8 us
    all_to_all x1, waiting for transfers between devices, every_slot(): values = exchange(v_cache, split_axis=1, concat_axis=0)  26.8 us
    all_to_all x1, waiting for transfers between devices, every_slot(): return keep_live(exchange(result, split_axis=0, concat_axis=1), tiles)  26.1 us
    another operation x1, loops' own time, every_slot(): result = lax.map(one, jnp.arange(N * ROWS // 512 * HEADS))  20.6 us
    dot_general x8, matrix products, one(): jnp.dot(weight, head_values, preferred_element_type=jnp.float32)  13.4 us
    reduce_sum x8, other arithmetic, one(): jnp.sum(weight, axis=-1, keepdims=True)  6.59 us
  transfers between devices with their start and end apart: 4, of which 4 were waited for; matrix products, arithmetic and copies ran while one was open for 1% of the time, Pallas kernels for 0%

profile of v2, /device:TPU:45, one launch (start us, length us, event | category | flops | bytes accessed | tf_op | source)
XLA Modules:
  0.0 298.2 jit_solution(6371248235309681102)
XLA Ops:
  0.0 103.9 %refresh_attention.1 = (bf16[128,4096]{1,0:T(8,128)(2,1)}, s32[1]{0:T(128)}) custom-call(s32[1,2]{1,0:T(1,128)} %tiles_ref.1, f32[8,128]{1,0:T(8,128)} %constant.96.clone.inv_ref, bf16[128,4096]{1,0:T(8,128)(2,1)} %q_ref.1, bf16[128,4096]{1,0:T(8,128)(2,1)} %k_ref.1, bf16[128,4096]{1,0:T(8,128)(2,1)} %v_ref.1), custom_call_target="tpu_custom_call" | custom-call | tf_op jit(solution)/shard_map/refresh_attention/pallas_call | solution.py:291
  103.9 192.0 %while.20 = (s32[]{:T(128)}, bf16[128,4096]{1,0:T(8,128)(2,1)}, bf16[128,4096]{1,0:T(8,128)(2,1)}, bf16[128,4096]{1,0:T(8,128)(2,1)}, bf16[128,4096]{1,0:T(8,128)(2,1)}, /*index=5*/s32[1,2]{1,0:T(1,128)}) while((s32[]{:T(128)}, bf16[128,4096]{1,0:T(8,128)(2,1)}, bf16[128,4096]{1,0:T(8,128)(2,1)}, bf16[128,4096]{1,0:T(8,128)(2,1)}, ...), condition=%region_5.6_spmd, body=%region_0.5_spmd | while | flops 551624448 | bytes 64372376 | solution.py:382
  104.8 0.7 multiply_bitcast_fusion
  105.6 1.4 convert_bitcast_fusion
  107.7 0.8 subtract_convert_fusion
  109.6 1.3 copy.14
  110.9 4.7 %all-to-all-start = ((bf16[128,16,256]{2,0,1:T(8,128)(2,1)}), bf16[128,16,256]{2,0,1:T(8,128)(2,1)S(1)}, u32[]{:S(2)}, u32[]{:S(2)}) async-start(bf16[128,16,256]{2,0,1:T(8,128)(2,1)} %copy.14), calls=%async_computation | async-start | bytes 2097152 | tf_op jit(solution)/shard_map/while/body/all_to_all | solution.py:357
  115.6 1.1 copy.26
  116.7 26.8 %all-to-all-done = bf16[128,16,256]{2,0,1:T(8,128)(2,1)S(1)} async-done(((bf16[128,16,256]{2,0,1:T(8,128)(2,1)}), bf16[128,16,256]{2,0,1:T(8,128)(2,1)S(1)}, u32[]{:S(2)}, u32[]{:S(2)}) %all-to-all-start) | async-done | bytes 1048608 | tf_op jit(solution)/shard_map/while/body/all_to_all | solution.py:357
  143.5 3.6 %all-to-all-start.2 = ((bf16[128,16,256]{2,0,1:T(8,128)(2,1)}), bf16[128,16,256]{2,0,1:T(8,128)(2,1)S(1)}, u32[]{:S(2)}, u32[]{:S(2)}) async-start(bf16[128,16,256]{2,0,1:T(8,128)(2,1)} %bitcast.34), calls=%async_computation.2 | async-start | bytes 2097152 | tf_op jit(solution)/shard_map/while/body/all_to_all | solution.py:348
  147.0 1.1 copy.27
  148.1 26.8 %all-to-all-done.2 = bf16[128,16,256]{2,0,1:T(8,128)(2,1)S(1)} async-done(((bf16[128,16,256]{2,0,1:T(8,128)(2,1)}), bf16[128,16,256]{2,0,1:T(8,128)(2,1)S(1)}, u32[]{:S(2)}, u32[]{:S(2)}) %all-to-all-start.2) | async-done | bytes 1048608 | tf_op jit(solution)/shard_map/while/body/all_to_all | solution.py:348
  174.9 3.6 %all-to-all-start.1 = ((bf16[128,16,256]{2,0,1:T(8,128)(2,1)}), bf16[128,16,256]{2,0,1:T(8,128)(2,1)S(1)}, u32[]{:S(2)}, u32[]{:S(2)}) async-start(bf16[128,16,256]{2,0,1:T(8,128)(2,1)} %bitcast.35), calls=%async_computation.1 | async-start | bytes 2097152 | tf_op jit(solution)/shard_map/while/body/all_to_all | solution.py:347
  178.5 27.9 %all-to-all-done.1 = bf16[128,16,256]{2,0,1:T(8,128)(2,1)S(1)} async-done(((bf16[128,16,256]{2,0,1:T(8,128)(2,1)}), bf16[128,16,256]{2,0,1:T(8,128)(2,1)S(1)}, u32[]{:S(2)}, u32[]{:S(2)}) %all-to-all-start.1) | async-done | bytes 1048608 | tf_op jit(solution)/shard_map/while/body/all_to_all | solution.py:347
  206.4 51.7 %while.21 = (s32[]{:T(128)}, bf16[8,512,128]{2,1,0:T(8,128)(2,1)}, s32[8]{0:T(128)S(1)}, bf16[2048,256]{1,0:T(8,128)(2,1)S(1)}, bf16[2048,256]{1,0:T(8,128)(2,1)...) while((s32[]{:T(128)}, bf16[8,512,128]{2,1,0:T(8,128)(2,1)}, ...), condition=%wide.region_4.4_spmd, body=%wide.region_1.3_spmd.sunk | while | flops 546372608 | bytes 13906303 | solution.py:369
  206.4 0.6 dynamic_slice.42
  209.6 0.8 multiply_reduce_fusion.2
  210.4 0.8 fusion.18
  211.2 1.7 fusion.19
  216.0 0.8 multiply_reduce_fusion.2
  216.8 0.8 fusion.18
  217.7 1.7 fusion.19
  222.5 0.8 multiply_reduce_fusion.2
  223.3 0.8 fusion.18
  224.1 1.7 fusion.19
  229.0 0.8 multiply_reduce_fusion.2
  229.8 0.8 fusion.18
  230.6 1.7 fusion.19
  232.3 0.6 dynamic_slice.42
  235.4 0.8 multiply_reduce_fusion.2
  236.2 0.8 fusion.18
  237.1 1.7 fusion.19
  241.9 0.8 multiply_reduce_fusion.2
  242.7 0.8 fusion.18
  243.5 1.7 fusion.19
  248.4 0.8 multiply_reduce_fusion.2
  249.2 0.8 fusion.18
  250.0 1.7 fusion.19
  254.8 0.8 multiply_reduce_fusion.2
  255.6 0.8 fusion.18
  256.5 1.7 fusion.19
  258.1 2.3 copy.28
  260.5 1.5 all_to_all.50
  262.0 3.6 %all-to-all-start.3 = ((bf16[16,128,256]{2,1,0:T(8,128)(2,1)}), bf16[16,128,256]{2,1,0:T(8,128)(2,1)S(1)}, u32[]{:S(2)}, u32[]{:S(2)}) async-start(bf16[16,128,256]{2,1,0:T(8,128)(2,1)} %all_to_all.50), calls=%async_computation.3 | async-start | bytes 2097152 | tf_op jit(solution)/shard_map/while/body/all_to_all | solution.py:371
  266.1 1.2 fusion.12
  267.3 26.1 %all-to-all-done.3 = bf16[16,128,256]{2,1,0:T(8,128)(2,1)S(1)} async-done(((bf16[16,128,256]{2,1,0:T(8,128)(2,1)}), bf16[16,128,256]{2,1,0:T(8,128)(2,1)S(1)}, u32[]{:S(2)}, u32[]{:S(2)}) %all-to-all-start.3) | async-done | bytes 1048608 | tf_op jit(solution)/shard_map/while/body/all_to_all | solution.py:371
  293.5 1.1 broadcast_select_fusion
  295.9 2.3 copy.45
  (23 shorter events, 6.1 us)
Async XLA Ops:
  108.5 7.0 %copy-start.1 = (bf16[128,4096]{1,0:T(8,128)(2,1)S(1)}, bf16[128,4096]{1,0:T(8,128)(2,1)}, u32[]{:S(2)}) copy-start(bf16[128,4096]{1,0:T(8,128)(2,1)} %get-tuple-element.113) | copy-start | bytes 3145732 | tf_op jit(solution)/shard_map/while
  109.5 37.5 %copy-start = (bf16[128,4096]{1,0:T(8,128)(2,1)S(1)}, bf16[128,4096]{1,0:T(8,128)(2,1)}, u32[]{:S(2)}) copy-start(bf16[128,4096]{1,0:T(8,128)(2,1)} %get-tuple-element.112) | copy-start | bytes 3145732 | tf_op jit(solution)/shard_map/while
  110.9 32.6 %all-to-all-start = ((bf16[128,16,256]{2,0,1:T(8,128)(2,1)}), bf16[128,16,256]{2,0,1:T(8,128)(2,1)S(1)}, u32[]{:S(2)}, u32[]{:S(2)}) async-start(bf16[128,16,256]{2,0,1:T(8,128)(2,1)} %copy.14), calls=%async_computation | async-start | bytes 2097152 | tf_op jit(solution)/shard_map/while/body/all_to_all | solution.py:357
  143.5 31.5 %all-to-all-start.2 = ((bf16[128,16,256]{2,0,1:T(8,128)(2,1)}), bf16[128,16,256]{2,0,1:T(8,128)(2,1)S(1)}, u32[]{:S(2)}, u32[]{:S(2)}) async-start(bf16[128,16,256]{2,0,1:T(8,128)(2,1)} %bitcast.34), calls=%async_computation.2 | async-start | bytes 2097152 | tf_op jit(solution)/shard_map/while/body/all_to_all | solution.py:348
  174.9 31.5 %all-to-all-start.1 = ((bf16[128,16,256]{2,0,1:T(8,128)(2,1)}), bf16[128,16,256]{2,0,1:T(8,128)(2,1)S(1)}, u32[]{:S(2)}, u32[]{:S(2)}) async-start(bf16[128,16,256]{2,0,1:T(8,128)(2,1)} %bitcast.35), calls=%async_computation.1 | async-start | bytes 2097152 | tf_op jit(solution)/shard_map/while/body/all_to_all | solution.py:347
  258.1 7.4 %copy-start.2 = (s32[1,2]{1,0:T(1,128)S(1)}, s32[1,2]{1,0:T(1,128)}, u32[]{:S(2)}) copy-start(s32[1,2]{1,0:T(1,128)} %get-tuple-element.110) | copy-start | bytes 28 | tf_op jit(solution)/shard_map/while
  262.0 31.5 %all-to-all-start.3 = ((bf16[16,128,256]{2,1,0:T(8,128)(2,1)}), bf16[16,128,256]{2,1,0:T(8,128)(2,1)S(1)}, u32[]{:S(2)}, u32[]{:S(2)}) async-start(bf16[16,128,256]{2,1,0:T(8,128)(2,1)} %all_to_all.50), calls=%async_computation.3 | async-start | bytes 2097152 | tf_op jit(solution)/shard_map/while/body/all_to_all | solution.py:371

commit v3 on v2

--- a/solution.py
+++ b/solution.py
@@ -23,11 +23,11 @@
 ROWS = SLOTS * TILE
 ROOM = {1: 8, 2: 6, 3: 5, 4: 3, 5: 1, 6: 0, 7: 0}
 HOPS = 5
-PACE = (12, 4, 4, 4, 4, 4)
+PACE = (10, 1)
 
 
 def kernel(tiles_ref, inv_ref, q_ref, k_ref, v_ref, o_ref, flag_ref,
-           q_in, q_out, q_chip, q_live, k_all, v_all, probs, norm, o_live, o_send,
+           q_in, q_out, q_chip, q_live, k_all, v_all, probs, norm, o_sum, o_live, o_send,
            count_out, count_all, counts,
            pack_a, pack_b, land_a, land_b,
            local_sem, count_ssem, count_rsem, twin_ssem, twin_rsem,
@@ -63,43 +63,6 @@
     count = jnp.full((8, DH), first_live + second_live, jnp.int32)
     count_out[...] = count
     count_all[me] = count
-    pl.semaphore_wait(barrier, N - 1)
-
-    def send_count(offset):
-        return remote(count_out, count_all.at[me], count_ssem.at[offset], count_rsem.at[offset], seq=peer(offset))
-
-    def send_k(offset):
-        to = peer(offset)
-        return remote(k_ref.at[:, at(to, LOCAL)], k_all.at[at(me, ROWS), :],
-                      k_ssem.at[offset], k_rsem.at[offset], seq=to)
-
-    def send_v(head, offset):
-        to = peer(offset)
-        return remote(v_ref.at[:, at(to * HEADS + head, DH)], v_all.at[at(me, ROWS), pl.ds(head * DH, DH)],
-                      v_ssem.at[head, offset], v_rsem.at[head, offset], seq=to)
-
-    def send_o(head, offset):
-        to = peer(offset)
-        return remote(o_send.at[offset, :, pl.ds(head * DH, DH)], o_ref.at[:, at(me * HEADS + head, DH)],
-                      o_ssem.at[head, offset], o_rsem.at[head, offset], seq=to)
-
-    order = []
-    for step in range(1, N // 2 + 1):
-        order += [step] if step == N // 2 else [step, N - step]
-    bulk = [send_k(offset) for offset in order]
-    bulk += [send_v(head, offset) for head in range(HEADS) for offset in order]
-    started = 0
-
-    def start_bulk(amount):
-        nonlocal started
-        for copy in bulk[started:started + amount]:
-            copy.start()
-        started += amount
-
-    for offset in order:
-        send_count(offset).start()
-    start_bulk(PACE[0])
-
     row = lax.broadcasted_iota(jnp.int32, (ROWS, DH), 0)
     lane = lax.broadcasted_iota(jnp.int32, (ROWS, DH), 1)
     first = jnp.maximum(tiles_ref[0, 0], 0) * TILE
@@ -122,8 +85,45 @@
 
     mine = q_chip.at[pl.ds(core * SLOTS, SLOTS)]
     lax.fori_loop(0, CHIPS * HEADS, functools.partial(rotate, 1 - core, q_out), 0)
+    pl.semaphore_wait(barrier, N - 1)
+
+    def send_count(offset):
+        return remote(count_out, count_all.at[me], count_ssem.at[offset], count_rsem.at[offset], seq=peer(offset))
+
+    def send_k(offset):
+        to = peer(offset)
+        return remote(k_ref.at[:, at(to, LOCAL)], k_all.at[at(me, ROWS), :],
+                      k_ssem.at[offset], k_rsem.at[offset], seq=to)
+
+    def send_v(head, offset):
+        to = peer(offset)
+        return remote(v_ref.at[:, at(to * HEADS + head, DH)], v_all.at[at(me, ROWS), pl.ds(head * DH, DH)],
+                      v_ssem.at[head, offset], v_rsem.at[head, offset], seq=to)
+
+    def send_o(head, offset):
+        to = peer(offset)
+        return remote(o_send.at[offset, :, pl.ds(head * DH, DH)], o_ref.at[:, at(me * HEADS + head, DH)],
+                      o_ssem.at[head, offset], o_rsem.at[head, offset], seq=to)
+
+    order = []
+    for step in range(1, N // 2 + 1):
+        order += [step] if step == N // 2 else [step, N - step]
+    bulk = [send_k(offset) for offset in order]
+    bulk += [send_v(head, offset) for head in range(HEADS) for offset in order]
+    started = 0
+
+    def start_bulk(amount):
+        nonlocal started
+        for copy in bulk[started:started + amount]:
+            copy.start()
+        started += amount
+
+    for offset in order:
+        send_count(offset).start()
     twin = remote(q_out, mine, twin_ssem.at[0], twin_rsem.at[0], seq=chip * 2 + 1 - core)
     twin.start()
+    start_bulk(PACE[0])
+
     lax.fori_loop(0, CHIPS * HEADS, functools.partial(rotate, core, mine), 0)
 
     for offset in order:
@@ -162,50 +162,52 @@
         index = jnp.where(rank < first_core[0], rank, rank + SLOTS - first_core[0])
         return jnp.clip(index, 0, 2 * SLOTS - 1)
 
-    def hop_a(hops):
-        return remote(pack_a.at[pl.ds(hops * 8, ROOM[hops])], land_a.at[pl.ds(hops * 8, ROOM[hops])],
-                      hop_ssem.at[0, hops], hop_rsem.at[0, hops], seq=peer(2))
-
-    def hop_b(hops):
-        return remote(pack_b.at[pl.ds(hops * 8, ROOM[hops])], land_b.at[pl.ds(hops * 8, ROOM[hops])],
-                      hop_ssem.at[1, hops], hop_rsem.at[1, hops], seq=peer(N - 2))
+    def hop(side, hops, head):
+        pack, land, to = ((pack_a, land_a, 2), (pack_b, land_b, N - 2))[side]
+        slots = pl.ds(hops * 8, ROOM[hops])
+        return remote(pack.at[head, slots], land.at[head, slots], hop_ssem.at[side, hops, head],
+                      hop_rsem.at[side, hops, head], seq=peer(to))
 
     twin.wait_recv()
     for hops in range(HOPS, 0, -1):
-        if hops < HOPS:
-            hop_a(hops + 1).wait_recv()
-            hop_b(hops + 1).wait_recv()
         to_a, to_b = hops, CHIPS - hops
-        column_a = at(lax.rem(chip + to_a, CHIPS), LOCAL)
-        column_b = at(lax.rem(chip + to_b, CHIPS), LOCAL)
-        for slot in range(ROOM[hops]):
-            rank = by_a[to_a] - 1 - slot - below[to_a][hops - 1]
-            value = q_chip[tile_at(rank), :, column_a]
-            if slot < ROOM[hops + 1]:
-                is_mine = jnp.logical_and(rank >= 0, rank < there[0])
-                value = jnp.where(is_mine, value, land_a[(hops + 1) * 8 + slot])
-            pack_a[hops * 8 + slot] = value
-            rank = by_b[to_b] - 1 - slot - above[to_b][hops - 1]
-            value = q_chip[tile_at(there[0] - 1 - rank), :, column_b]
-            if slot < ROOM[hops + 1]:
-                is_mine = jnp.logical_and(rank >= 0, rank < there[0])
-                value = jnp.where(is_mine, value, land_b[(hops + 1) * 8 + slot])
-            pack_b[hops * 8 + slot] = value
-        hop_a(hops).start()
-        hop_b(hops).start()
-        start_bulk(PACE[HOPS + 1 - hops])
+        for head in range(HEADS):
+            if hops < HOPS:
+                hop(0, hops + 1, head).wait_recv()
+                hop(1, hops + 1, head).wait_recv()
+            column_a = at(lax.rem(chip + to_a, CHIPS) * HEADS + head, DH)
+            column_b = at(lax.rem(chip + to_b, CHIPS) * HEADS + head, DH)
+            for slot in range(ROOM[hops]):
+                rank = by_a[to_a] - 1 - slot - below[to_a][hops - 1]
+                value = q_chip[tile_at(rank), :, column_a]
+                if slot < ROOM[hops + 1]:
+                    is_mine = jnp.logical_and(rank >= 0, rank < there[0])
+                    value = jnp.where(is_mine, value, land_a[head, (hops + 1) * 8 + slot])
+                pack_a[head, hops * 8 + slot] = value
+                rank = by_b[to_b] - 1 - slot - above[to_b][hops - 1]
+                value = q_chip[tile_at(there[0] - 1 - rank), :, column_b]
+                if slot < ROOM[hops + 1]:
+                    is_mine = jnp.logical_and(rank >= 0, rank < there[0])
+                    value = jnp.where(is_mine, value, land_b[head, (hops + 1) * 8 + slot])
+                pack_b[head, hops * 8 + slot] = value
+            hop(0, hops, head).start()
+            hop(1, hops, head).start()
+            start_bulk(PACE[1])
     start_bulk(len(bulk) - started)
 
-    hop_a(1).wait_recv()
-    hop_b(1).wait_recv()
-    column = at(chip, LOCAL)
-    for slot in range(LIVE):
-        value = q_chip[tile_at(slot - total[0]), :, column]
-        other = land_b[8 + jnp.clip(slot - by_a[0], 0, 7)]
-        value = jnp.where(slot < total[0], other, value)
-        if slot < ROOM[1]:
-            value = jnp.where(slot < by_a[0], land_a[8 + slot], value)
-        q_live[slot * TILE:(slot + 1) * TILE, :] = value
+    for head in range(HEADS):
+        hop(0, 1, head).wait_recv()
+        hop(1, 1, head).wait_recv()
+    for head in range(HEADS):
+        column = at(chip * HEADS + head, DH)
+        columns = pl.ds(head * DH, DH)
+        for slot in range(LIVE):
+            value = q_chip[tile_at(slot - total[0]), :, column]
+            other = land_b[head, 8 + jnp.clip(slot - by_a[0], 0, 7)]
+            value = jnp.where(slot < total[0], other, value)
+            if slot < ROOM[1]:
+                value = jnp.where(slot < by_a[0], land_a[head, 8 + slot], value)
+            q_live[slot * TILE:(slot + 1) * TILE, columns] = value
 
     own_k.wait()
     for offset in order:
@@ -231,36 +233,42 @@
 
     lax.fori_loop(0, LIVE * TILE // block, score, 0)
 
+    places = {}
+    for offset in order + [0]:
+        home = peer(offset)
+        back = CHIPS - lax.rem(home // 2 - chip + CHIPS, CHIPS)
+        before = jnp.int32(0)
+        for step in range(1, CHIPS):
+            before = jnp.where(back == step, below[0][step - 1], before)
+        rank = jnp.where(lax.rem(home, 2) == 0, 0, counts[home // 2 * 2, 0, 0])
+        for slot in range(SLOTS):
+            index = before + rank + slot
+            index = jnp.where(index < by_a[0], by_a[0] - 1 - index, index)
+            index = jnp.where(back == CHIPS, total[0] + rank + slot, index)
+            places[offset, slot] = jnp.clip(index, 0, LIVE - 1)
+
     own_v.wait()
     for head in range(HEADS):
         columns = pl.ds(head * DH, DH)
-        for offset in order:
-            send_v(head, offset).wait_recv()
-
-        def combine(index, carry):
-            product = jnp.dot(
-                probs[head, at(index, block), :], v_all[:, columns], preferred_element_type=jnp.float32
-            )
-            product = (product * norm[at(index, block), columns]).astype(jnp.bfloat16)
-            for part in range(2):
-                o_live[head, index * 2 + part] = product[part * TILE:(part + 1) * TILE, :]
-            return carry
-
-        lax.fori_loop(0, LIVE * TILE // block, combine, 0)
+        for step, away in enumerate((0, 1, 7, 2, 6, 3, 5, 4)):
+            if away == 0:
+                send_v(head, lax.rem(N + 2 * core - 1, N)).wait_recv()
+            else:
+                for which in range(2):
+                    send_v(head, 2 * away + core - which).wait_recv()
+            rows = at(lax.rem(chip - away + CHIPS, CHIPS), 2 * ROWS)
+            product = jnp.dot(probs[head, :, rows], v_all[rows, columns], preferred_element_type=jnp.float32)
+            if step == 0:
+                o_sum[...] = product
+            elif step < CHIPS - 1:
+                o_sum[...] += product
+            else:
+                product = ((o_sum[...] + product) * norm[:, columns]).astype(jnp.bfloat16)
+                for slot in range(LIVE):
+                    o_live[head, slot] = product[slot * TILE:(slot + 1) * TILE, :]
         for offset in order + [0]:
-            home = peer(offset)
-            away = lax.rem(home // 2 - chip + CHIPS, CHIPS)
-            which = lax.rem(home, 2)
-            back = (CHIPS - away)
-            before = jnp.int32(0)
-            for step in range(1, CHIPS):
-                before = jnp.where(back == step, below[0][step - 1], before)
-            rank = jnp.where(which == 0, 0, counts[home // 2 * 2, 0, 0])
             for slot in range(SLOTS):
-                index = before + rank + slot
-                index = jnp.where(index < by_a[0], by_a[0] - 1 - index, index)
-                index = jnp.where(back == CHIPS, total[0] + rank + slot, index)
-                o_send[offset, slot * TILE:(slot + 1) * TILE, columns] = o_live[head, jnp.clip(index, 0, LIVE - 1)]
+                o_send[offset, slot * TILE:(slot + 1) * TILE, columns] = o_live[head, places[offset, slot]]
             if offset > 0:
                 send_o(head, offset).start()
     o_ref[:, at(me, LOCAL)] = o_send[0]
@@ -269,8 +277,9 @@
         send_count(offset).wait_send()
     twin.wait_send()
     for hops in range(1, HOPS + 1):
-        hop_a(hops).wait_send()
-        hop_b(hops).wait_send()
+        for head in range(HEADS):
+            hop(0, hops, head).wait_send()
+            hop(1, hops, head).wait_send()
     for copy in bulk:
         copy.wait_send()
     for head in range(HEADS):
@@ -287,7 +296,7 @@
     inverse = jnp.asarray(np.broadcast_to(np.tile(inverse, 2)[None, :], (8, DH)), jnp.float32)
     dma = pltpu.SemaphoreType.DMA
     bf16, i32 = jnp.bfloat16, jnp.int32
-    unit = (TILE, LOCAL)
+    packets = pltpu.VMEM((HEADS, (HOPS + 1) * 8, TILE, DH), bf16)
     return pl.pallas_call(
         kernel,
         out_shape=(
@@ -311,19 +320,17 @@
             pltpu.VMEM((N * ROWS, LOCAL), bf16),
             pltpu.VMEM((HEADS, LIVE * TILE, N * ROWS), bf16),
             pltpu.VMEM((LIVE * TILE, LOCAL), jnp.float32),
+            pltpu.VMEM((LIVE * TILE, DH), jnp.float32),
             pltpu.VMEM((HEADS, LIVE, TILE, DH), bf16),
             pltpu.VMEM((N, ROWS, LOCAL), bf16),
             pltpu.VMEM((8, DH), i32),
             pltpu.VMEM((N, 8, DH), i32),
             pltpu.SMEM((N, 8, DH), i32),
-            pltpu.VMEM(((HOPS + 1) * 8,) + unit, bf16),
-            pltpu.VMEM(((HOPS + 1) * 8,) + unit, bf16),
-            pltpu.VMEM(((HOPS + 1) * 8,) + unit, bf16),
-            pltpu.VMEM(((HOPS + 1) * 8,) + unit, bf16),
+            packets, packets, packets, packets,
             dma((4,)),
             dma((N,)), dma((N,)),
             dma((1,)), dma((1,)),
-            dma((2, HOPS + 1)), dma((2, HOPS + 1)),
+            dma((2, HOPS + 1, HEADS)), dma((2, HOPS + 1, HEADS)),
             dma((N,)), dma((N,)),
             dma((HEADS, N)), dma((HEADS, N)),
             dma((HEADS, N)), dma((HEADS, N)),
@@ -373,13 +380,12 @@
 
 def on_device(q_slots, k_cache, v_cache, tiles):
     attended, misfit = refresh(q_slots, k_cache, v_cache, tiles)
-    def other_way(carry):
+    def other_way():
         rowwise = Layout(major_to_minor=(0, 1))
-        _, *given = lax.optimization_barrier((carry[0], q_slots, k_cache, v_cache, tiles))
-        given = [with_layout_constraint(array, rowwise) for array in given]
-        return jnp.int32(0), with_layout_constraint(every_slot(*given), rowwise)
-
-    return lax.while_loop(lambda carry: carry[0] > 0, other_way, (misfit[0], attended))[1]
+        given = [with_layout_constraint(array, rowwise) for array in (q_slots, k_cache, v_cache, tiles)]
+        return with_layout_constraint(every_slot(*given), rowwise)
+
+    return lax.cond(misfit[0] > 0, other_way, lambda: attended)
 
 
 def solution(mesh):

time: 299 us -> 104 us (0.35)
  the two profiles are of different devices: /device:TPU:45 before, /device:TPU:1 now
where the time goes in v3:
time: 104 us; the launch traced here: 103 us
  Pallas kernels  102 us (98%)
    pallas_call x1, Pallas kernels, refresh(): pl.pallas_call(kernel, out_shape=(jax.ShapeDtypeStruct((ROWS, width), bf1...  102 us

profile of v3, /device:TPU:1, one launch (start us, length us, event | category | flops | bytes accessed | tf_op | source)
XLA Modules:
  0.0 103.3 jit_solution(13089947160561303502)
XLA Ops:
  0.0 101.5 %refresh_attention.1 = (bf16[128,4096]{1,0:T(8,128)(2,1)S(1)}, s32[1]{0:T(128)}) custom-call(s32[1,2]{1,0:T(1,128)} %tiles_ref.1, f32[8,128]{1,0:T(8,128)} %constant.97.clone.inv_ref, bf16[128,4096]{1,0:T(8,128)(2,1)} %q_ref.1, bf16[128,4096]{1,0:T(8,128)(2,1)} %k_ref.1, bf16[128,4096]{1,0:T(8,128)(2,1)} %v_ref.1), custom_call_target="tpu_custom_call" | custom-call | tf_op jit(solution)/shard_map/refresh_attention/pallas_call | solution.py:300
  102.1 0.2 conditional.1
  102.3 1.0 copy.41

commit v4 on v3

--- a/solution.py
+++ b/solution.py
@@ -26,8 +26,8 @@
 PACE = (10, 1)
 
 
-def kernel(tiles_ref, inv_ref, q_ref, k_ref, v_ref, o_ref, flag_ref,
-           q_in, q_out, q_chip, q_live, k_all, v_all, probs, norm, o_sum, o_live, o_send,
+def kernel(tiles_in, inv_in, q_ref, k_ref, v_ref, o_ref, flag_ref,
+           tiles_ref, inv_ref, q_in, q_out, q_chip, q_live, k_all, v_all, probs, norm, o_sum, o_live, o_send,
            count_out, count_all, counts,
            pack_a, pack_b, land_a, land_b,
            local_sem, count_ssem, count_rsem, twin_ssem, twin_rsem,
@@ -51,6 +51,10 @@
     barrier = pltpu.get_barrier_semaphore()
     for offset in range(1, N):
         pl.semaphore_signal(barrier, inc=1, device_id={"seq": peer(offset)}, device_id_type=MESH)
+    load_tiles = pltpu.make_async_copy(tiles_in, tiles_ref, local_sem.at[4])
+    load_tiles.start()
+    load_inv = pltpu.make_async_copy(inv_in, inv_ref, local_sem.at[5])
+    load_inv.start()
     load_q = pltpu.make_async_copy(q_ref, q_in, local_sem.at[0])
     load_q.start()
     own_k = pltpu.make_async_copy(k_ref.at[:, at(me, LOCAL)], k_all.at[at(me, ROWS), :], local_sem.at[1])
@@ -58,6 +62,7 @@
     own_v = pltpu.make_async_copy(v_ref.at[:, at(me, LOCAL)], v_all.at[at(me, ROWS), :], local_sem.at[2])
     own_v.start()
 
+    load_tiles.wait()
     first_live = (tiles_ref[0, 0] >= 0).astype(jnp.int32)
     second_live = (tiles_ref[0, 1] >= 0).astype(jnp.int32)
     count = jnp.full((8, DH), first_live + second_live, jnp.int32)
@@ -68,6 +73,7 @@
     first = jnp.maximum(tiles_ref[0, 0], 0) * TILE
     second = (jnp.maximum(tiles_ref[0, 1], 0) - 1) * TILE
     position = (me * ROWS + row + jnp.where(row < TILE, first, second)).astype(jnp.float32)
+    load_inv.wait()
     angles = position * inv_ref[0:1, :]
     cosine = jnp.cos(angles)
     sine = jnp.sin(angles)
@@ -304,14 +310,16 @@
             jax.ShapeDtypeStruct((1,), i32),
         ),
         in_specs=[
-            pl.BlockSpec(memory_space=pltpu.SMEM),
-            pl.BlockSpec(memory_space=pltpu.VMEM),
+            pl.BlockSpec(memory_space=pl.ANY),
+            pl.BlockSpec(memory_space=pl.ANY),
             pl.BlockSpec(memory_space=pl.ANY),
             pl.BlockSpec(memory_space=pl.ANY),
             pl.BlockSpec(memory_space=pl.ANY),
         ],
         out_specs=(pl.BlockSpec(memory_space=pltpu.VMEM), pl.BlockSpec(memory_space=pltpu.SMEM)),
         scratch_shapes=[
+            pltpu.SMEM((1, SLOTS), i32),
+            pltpu.VMEM((8, DH), jnp.float32),
             pltpu.VMEM((ROWS, width), bf16),
             pltpu.VMEM((SLOTS, TILE, width // 2), bf16),
             pltpu.VMEM((2 * SLOTS, TILE, width // 2), bf16),
@@ -327,7 +335,7 @@
             pltpu.VMEM((N, 8, DH), i32),
             pltpu.SMEM((N, 8, DH), i32),
             packets, packets, packets, packets,
-            dma((4,)),
+            dma((6,)),
             dma((N,)), dma((N,)),
             dma((1,)), dma((1,)),
             dma((2, HOPS + 1, HEADS)), dma((2, HOPS + 1, HEADS)),

time: 104 us -> 104 us (level)
  no operation moved by 1% of the time
where the time goes in v4:
time: 104 us; the launch traced here: 103 us
  Pallas kernels  101 us (97%)
    pallas_call x1, Pallas kernels, refresh(): pl.pallas_call(kernel, out_shape=(jax.ShapeDtypeStruct((ROWS, width), bf1...  101 us

profile of v4, /device:TPU:1, one launch (start us, length us, event | category | flops | bytes accessed | tf_op | source)
XLA Modules:
  0.0 102.8 jit_solution(18247112457613838630)
XLA Ops:
  0.0 101.0 %refresh_attention.1 = (bf16[128,4096]{1,0:T(8,128)(2,1)S(1)}, s32[1]{0:T(128)}) custom-call(s32[1,2]{1,0:T(1,128)} %tiles_in.1, f32[8,128]{1,0:T(8,128)} %constant.97.clone.inv_in, bf16[128,4096]{1,0:T(8,128)(2,1)} %q_ref.1, bf16[128,4096]{1,0:T(8,128)(2,1)} %k_ref.1, bf16[128,4096]{1,0:T(8,128)(2,1)} %v_ref.1), custom_call_target="tpu_custom_call" | custom-call | tf_op jit(solution)/shard_map/refresh_attention/pallas_call | solution.py:306
  101.6 0.2 conditional.1
  101.8 1.0 copy.41

commit v5 on v4

--- a/solution.py
+++ b/solution.py
@@ -21,7 +21,7 @@
 N = 16
 CHIPS = N // 2
 ROWS = SLOTS * TILE
-ROOM = {1: 8, 2: 6, 3: 5, 4: 3, 5: 1, 6: 0, 7: 0}
+ROOM = {1: 8, 2: 7, 3: 5, 4: 3, 5: 2, 6: 0, 7: 0}
 HOPS = 5
 PACE = (10, 1)
 

time: 104 us -> 104 us (level); the launches traced: 103 us -> 104 us
    pallas_call x1, Pallas kernels: 101 us -> 102 us  [refresh(): pl.pallas_call(kernel, out_shape=(jax.ShapeDtypeStruct((ROWS, width), bf1...]
where the time goes in v5:
time: 104 us
  Pallas kernels  102 us (98%)
    pallas_call x1, Pallas kernels, refresh(): pl.pallas_call(kernel, out_shape=(jax.ShapeDtypeStruct((ROWS, width), bf1...  102 us

profile of v5, /device:TPU:1, one launch (start us, length us, event | category | flops | bytes accessed | tf_op | source)
XLA Modules:
  0.0 104.2 jit_solution(12827417161850460186)
XLA Ops:
  0.0 102.5 %refresh_attention.1 = (bf16[128,4096]{1,0:T(8,128)(2,1)S(1)}, s32[1]{0:T(128)}) custom-call(s32[1,2]{1,0:T(1,128)} %tiles_in.1, f32[8,128]{1,0:T(8,128)} %constant.97.clone.inv_in, bf16[128,4096]{1,0:T(8,128)(2,1)} %q_ref.1, bf16[128,4096]{1,0:T(8,128)(2,1)} %k_ref.1, bf16[128,4096]{1,0:T(8,128)(2,1)} %v_ref.1), custom_call_target="tpu_custom_call" | custom-call | tf_op jit(solution)/shard_map/refresh_attention/pallas_call | solution.py:306
  103.0 0.2 conditional.1
  103.3 1.0 copy.41

commit v6 on v5

--- a/solution.py
+++ b/solution.py
@@ -23,7 +23,7 @@
 ROWS = SLOTS * TILE
 ROOM = {1: 8, 2: 7, 3: 5, 4: 3, 5: 2, 6: 0, 7: 0}
 HOPS = 5
-PACE = (10, 1)
+PACE = (8, 1)
 
 
 def kernel(tiles_in, inv_in, q_ref, k_ref, v_ref, o_ref, flag_ref,
@@ -239,9 +239,10 @@
 
     lax.fori_loop(0, LIVE * TILE // block, score, 0)
 
-    places = {}
+    places, alive = {}, {}
     for offset in order + [0]:
         home = peer(offset)
+        alive[offset] = counts[home, 0, 0]
         back = CHIPS - lax.rem(home // 2 - chip + CHIPS, CHIPS)
         before = jnp.int32(0)
         for step in range(1, CHIPS):
@@ -274,7 +275,9 @@
                     o_live[head, slot] = product[slot * TILE:(slot + 1) * TILE, :]
         for offset in order + [0]:
             for slot in range(SLOTS):
-                o_send[offset, slot * TILE:(slot + 1) * TILE, columns] = o_live[head, places[offset, slot]]
+                value = o_live[head, places[offset, slot]]
+                value = jnp.where(slot < alive[offset], value, jnp.zeros((), jnp.bfloat16))
+                o_send[offset, slot * TILE:(slot + 1) * TILE, columns] = value
             if offset > 0:
                 send_o(head, offset).start()
     o_ref[:, at(me, LOCAL)] = o_send[0]
@@ -291,9 +294,6 @@
     for head in range(HEADS):
         for offset in order:
             send_o(head, offset).wait()
-    for slot in range(SLOTS):
-        rows = pl.ds(slot * TILE, TILE)
-        o_ref[rows, :] = jnp.where(tiles_ref[0, slot] >= 0, o_ref[rows, :], jnp.zeros((), jnp.bfloat16))
 
 
 def refresh(q_slots, k_cache, v_cache, tiles):

time: 104 us -> 104 us (level)
  no operation moved by 1% of the time
where the time goes in v6:
time: 104 us
  Pallas kernels  102 us (98%)
    pallas_call x1, Pallas kernels, refresh(): pl.pallas_call(kernel, out_shape=(jax.ShapeDtypeStruct((ROWS, width), bf1...  102 us

profile of v6, /device:TPU:1, one launch (start us, length us, event | category | flops | bytes accessed | tf_op | source)
XLA Modules:
  0.0 104.1 jit_solution(2642942623591291133)
XLA Ops:
  0.0 102.4 %refresh_attention.1 = (bf16[128,4096]{1,0:T(8,128)(2,1)S(1)}, s32[1]{0:T(128)}) custom-call(s32[1,2]{1,0:T(1,128)} %tiles_in.1, f32[8,128]{1,0:T(8,128)} %constant.97.clone.inv_in, bf16[128,4096]{1,0:T(8,128)(2,1)} %q_ref.1, bf16[128,4096]{1,0:T(8,128)(2,1)} %k_ref.1, bf16[128,4096]{1,0:T(8,128)(2,1)} %v_ref.1), custom_call_target="tpu_custom_call" | custom-call | tf_op jit(solution)/shard_map/refresh_attention/pallas_call | solution.py:306
  102.9 0.2 conditional.1
  103.2 1.0 copy.41
